TPU v7x, 1024 devices: a whole 4x8x16 slice. The times are simulated.
1024 devices in a mesh: tile: 128 (over y, x, z_hi), tracer: 8 (over z_lo, core).
Axes of the slice: x: 4, y: 8, z: 16 (z_hi: 4, z_lo: 4; z = z_hi * 4 + z_lo), core: 2. Of those that a mesh axis runs over, the one named last changes fastest.
Arguments:
- tracers: float32 [96, 8, 1024, 128], P('tracer', None, 'tile'), may hold values from 0.2 to 5
- courant_x: float32 [8, 1024, 128], P('tracer', 'tile'), may hold values from -0.45 to 0.45
- courant_y: float32 [8, 1024, 128], P('tracer', 'tile'), may hold values from -0.45 to 0.45
- kdiff: float32 [8, 1024, 128], P('tracer', 'tile'), may hold values from 0.05 to 4
- humidity: float32 [8, 1024, 128], P('tracer', 'tile'), may hold values from 0 to 0.9
- land: int32 [1024, 128], P('tile'), may hold values 0 or 1
- band_class: int32 [96], replicated, may hold values from 0 to 7
- opt_table: float32 [8, 14], replicated, may hold values from 0.002 to 0.02
- hyg_table: float32 [8], replicated, may hold values from 0.2 to 1
Outputs:
- tracers_out: float32 [96, 8, 1024, 128], P('tracer', None, 'tile')
- extinction: float32 [8, 14, 1024, 128], P('tracer', None, 'tile')
Inputs may be any that keep to these rules, and one draw needn't show every extreme that they name: land holds only 0 and 1. band_class indexes rows of opt_table and hyg_table.
All inputs are finite; a program needn't handle non-finite values. No bound on the sum of `land` on one device may be relied on, other than what follows from the above.
Results may differ from a plain program's by a relative error of at most 0.0003.
Values sent between devices are 32-bit elements; how exact they have to be, the bound alone decides.
A program may use at most 32 MiB of HBM per device.

v0:
```python
import jax
import jax.numpy as jnp
from jax import lax
from jax.sharding import PartitionSpec as P


def with_halo(block, sides, width):
    for axis, dim in sides:
        count = lax.axis_size(axis)
        forward = [(i, i + 1) for i in range(count - 1)]
        forward.append((count - 1, 0))
        backward = [(target, source) for source, target in forward]
        low = lax.ppermute(
            lax.slice_in_dim(block, block.shape[dim] - width, None, axis=dim), axis, forward
        )
        high = lax.ppermute(lax.slice_in_dim(block, 0, width, axis=dim), axis, backward)
        block = jnp.concatenate([low, block, high], axis=dim)
    return block


def minmod(left_step, right_step):
    return (
        0.5
        * (jnp.sign(left_step) + jnp.sign(right_step))
        * jnp.minimum(jnp.abs(left_step), jnp.abs(right_step))
    )


def flux_divergence(values, courant, along):
    behind = jnp.roll(values, 1, along)
    leading = jnp.roll(values, -1, along)
    slopes = minmod(values - behind, leading - values)
    face_value = jnp.where(
        courant >= 0,
        behind + 0.5 * (1.0 - courant) * jnp.roll(slopes, 1, along),
        values - 0.5 * (1.0 + courant) * slopes,
    )
    fluxes = courant * face_value
    return jnp.roll(fluxes, -1, along) - fluxes


def column_solve(values, coupling):
    levels_total = coupling.shape[0]
    upper_coef = []
    forward = []
    previous_upper = None
    previous_solved = None
    for height in range(levels_total):
        lower_link = coupling[height]
        source = values[..., height, :, :]
        if height == 0:
            divisor = 1.0 + lower_link
            solved = source / divisor
        else:
            upper_link = coupling[height - 1]
            divisor = 1.0 + upper_link + lower_link + upper_link * previous_upper
            solved = (source + upper_link * previous_solved) / divisor
        previous_upper = -lower_link / divisor
        previous_solved = solved
        upper_coef.append(previous_upper)
        forward.append(solved)
    result = [forward[-1]] * levels_total
    current = forward[-1]
    for height in range(levels_total - 2, -1, -1):
        current = forward[height] - upper_coef[height] * current
        result[height] = current
    return jnp.stack(result, axis=-3)


def advect(values, wind_east, wind_north):
    full_width = values.shape[2]
    jumps_east = values[:, :, 1:] - values[:, :, :-1]
    slopes = minmod(jumps_east[:, :, :-1], jumps_east[:, :, 1:])
    courant = wind_east[:, 2 : full_width - 1]
    face_value = jnp.where(
        courant >= 0,
        values[:, :, 1 : full_width - 2] + 0.5 * (1.0 - courant) * slopes[:, :, : full_width - 3],
        values[:, :, 2 : full_width - 1] - 0.5 * (1.0 + courant) * slopes[:, :, 1 : full_width - 2],
    )
    fluxes = courant * face_value
    center = values[:, :, 2 : full_width - 2]
    return center - (fluxes[:, :, 1:] - fluxes[:, :, :-1]) - flux_divergence(center, wind_north, 3)


def local(tracers, courant_x, courant_y, kdiff, humidity, land, band_class, opt_table, hyg_table):
    wind_east, wind_north, mixing, moisture = (
        lax.all_gather(courant_x, "tracer", axis=0, tiled=True),
        lax.all_gather(courant_y, "tracer", axis=0, tiled=True),
        lax.all_gather(kdiff, "tracer", axis=0, tiled=True),
        lax.all_gather(humidity, "tracer", axis=0, tiled=True),
    )
    surface = mixing[-1:] * (0.25 + 0.75 * land.astype(jnp.float32))[None]
    coupling = jnp.concatenate([mixing[:-1], surface], 0)

    def advance(state):
        stacked = jnp.concatenate([state, wind_east[None]], 0)
        padded = with_halo(stacked, (("tile", 2),), 2)
        moved = advect(padded[:-1], padded[-1], wind_north)
        return column_solve(moved, coupling)

    middle = advance(tracers)
    final = advance(middle)
    group_size = tracers.shape[0]
    first_tracer = lax.axis_index("tracer") * group_size
    local_class = lax.dynamic_slice_in_dim(band_class, first_tracer, group_size, 0)
    classes = jnp.arange(hyg_table.shape[0], dtype=jnp.int32)
    selector = (local_class[:, None] == classes[None, :]).astype(jnp.float32)
    growth_rate = jnp.dot(
        selector, hyg_table, precision=lax.Precision.HIGHEST, preferred_element_type=jnp.float32
    )
    dryness = jnp.log(1.0 - moisture)
    swelling = jnp.exp(-growth_rate[:, None, None, None] * dryness[None])
    wetted = final * swelling
    optics = jnp.dot(
        selector, opt_table, precision=lax.Precision.HIGHEST, preferred_element_type=jnp.float32
    )
    partial_sum = jnp.einsum("tlxy,tb->lbxy", wetted, optics, precision=lax.Precision.HIGHEST)
    extinction = lax.psum_scatter(partial_sum, "tracer", scatter_dimension=0, tiled=True)
    return (final, extinction)


def solution(mesh):
    in_specs = (
        P("tracer", None, "tile", None),
        P("tracer", "tile", None),
        P("tracer", "tile", None),
        P("tracer", "tile", None),
        P("tracer", "tile", None),
        P("tile", None),
        P(),
        P(),
        P(),
    )
    out_specs = (P("tracer", None, "tile", None), P("tracer", None, "tile", None))
    return jax.shard_map(local, mesh=mesh, in_specs=in_specs, out_specs=out_specs, check_vma=False)
```

profile of v0, /device:TPU:1, one launch (start us, length us, event | category | flops | bytes accessed | tf_op | source)
XLA Modules:
  0.0 176.2 jit_solution(13902748669018801069)
XLA Ops:
  7.2 28.2 %all_gather.12 = f32[8,8,128]{2,1,0:T(8,128)S(1)} all-gather(f32[1,8,128]{2,1,0:T(8,128)} %param.10), channel_id=1, replica_groups=mesh['tile'=128,'tracer'=8] {'tracer'}, dimensions={0}, use_global_device_ids=true | all-gather | bytes 36864 | tf_op jit(solution)/shard_map/all_gather | solution.py:87
  35.5 1.2 fusion.29
  36.7 10.4 %collective-permute-start.1 = (f32[13,8,2,128]{3,2,1,0:T(2,128)S(1)}, f32[13,8,2,128]{3,2,1,0:T(2,128)S(1)}, u32[]{:S(2)}, u32[]{:S(2)}) collective-permute-start(f32[13,8,2,128]{3,2,1,0:T(2,128)S(1)} %get-tuple-element.32), channel_id=1, source_target_pairs={{8,0},{16,8},{24,16},{32,24},{40,32},{48,40},{56,48},{64,56},{72,6... | collective-permute-start | bytes 319496 | tf_op jit(solution)/shard_map/ppermute | solution.py:16
  47.0 1.9 %collective-permute-start = (f32[13,8,2,128]{3,2,1,0:T(2,128)S(1)}, f32[13,8,2,128]{3,2,1,0:T(2,128)S(1)}, u32[]{:S(2)}, u32[]{:S(2)}) collective-permute-start(f32[13,8,2,128]{3,2,1,0:T(2,128)S(1)} %get-tuple-element.31), channel_id=1, source_target_pairs={{0,8},{8,16},{16,24},{24,32},{32,40},{40,48},{48,56},{56,64},{64,7... | collective-permute-start | bytes 319496 | tf_op jit(solution)/shard_map/ppermute | solution.py:13
  49.4 0.5 copy-done.3
  49.9 15.8 %all_gather.13 = f32[8,8,128]{2,1,0:T(8,128)S(1)} all-gather(f32[1,8,128]{2,1,0:T(8,128)S(1)} %copy-done.3), channel_id=1, replica_groups=mesh['tile'=128,'tracer'=8] {'tracer'}, dimensions={0}, use_global_device_ids=true | all-gather | bytes 36864 | tf_op jit(solution)/shard_map/all_gather | solution.py:88
  65.7 0.7 copy-done.4
  66.3 14.0 %all_gather.14 = f32[8,8,128]{2,1,0:T(8,128)S(1)} all-gather(f32[1,8,128]{2,1,0:T(8,128)S(1)} %copy-done.4), channel_id=1, replica_groups=mesh['tile'=128,'tracer'=8] {'tracer'}, dimensions={0}, use_global_device_ids=true | all-gather | bytes 36864 | tf_op jit(solution)/shard_map/all_gather | solution.py:89
  80.4 0.4 minimum_multiply_fusion.3
  81.5 0.7 copy-done.5
  82.2 14.0 %all_gather.15 = f32[8,8,128]{2,1,0:T(8,128)S(1)} all-gather(f32[1,8,128]{2,1,0:T(8,128)S(1)} %copy-done.5), channel_id=1, replica_groups=mesh['tile'=128,'tracer'=8] {'tracer'}, dimensions={0}, use_global_device_ids=true | all-gather | bytes 36864 | tf_op jit(solution)/shard_map/all_gather | solution.py:90
  96.2 0.7 copy-done.7
  97.0 0.6 copy-done.8
  98.3 0.6 minimum_multiply_fusion.1
  98.9 0.4 fusion.8
  100.2 11.6 %collective-permute-start.3 = (f32[13,8,2,128]{3,2,1,0:T(2,128)S(1)}, f32[13,8,2,128]{3,2,1,0:T(2,128)S(1)}, u32[]{:S(2)}, u32[]{:S(2)}) collective-permute-start(f32[13,8,2,128]{3,2,1,0:T(2,128)S(1)} %get-tuple-element.30), channel_id=1, source_target_pairs={{8,0},{16,8},{24,16},{32,24},{40,32},{48,40},{56,48},{64,56},{72,6... | collective-permute-start | bytes 319496 | tf_op jit(solution)/shard_map/ppermute | solution.py:16
  111.7 1.9 %collective-permute-start.2 = (f32[13,8,2,128]{3,2,1,0:T(2,128)S(1)}, f32[13,8,2,128]{3,2,1,0:T(2,128)S(1)}, u32[]{:S(2)}, u32[]{:S(2)}) collective-permute-start(f32[13,8,2,128]{3,2,1,0:T(2,128)S(1)} %get-tuple-element.29), channel_id=1, source_target_pairs={{0,8},{8,16},{16,24},{24,32},{32,40},{40,48},{48,56},{56,64},{64,7... | collective-permute-start | bytes 319496 | tf_op jit(solution)/shard_map/ppermute | solution.py:13
  113.7 0.4 minimum_multiply_fusion.2
  114.8 11.7 %collective-permute-done.2 = f32[13,8,2,128]{3,2,1,0:T(2,128)S(1)} collective-permute-done((f32[13,8,2,128]{3,2,1,0:T(2,128)S(1)}, f32[13,8,2,128]{3,2,1,0:T(2,128)S(1)}, u32[]{:S(2)}, u32[]{:S(2)}) %collective-permute-start.2) | collective-permute-done | bytes 106528 | tf_op jit(solution)/shard_map/ppermute | solution.py:13
  126.8 0.6 minimum_multiply_fusion
  128.3 0.6 copy-done.2
  128.9 1.6 convolution_bitcast_fusion
  130.5 37.3 %reduce-scatter.2.cloned.1.call-done = f32[1,14,8,128]{3,1,2,0:T(8,128)} async-done(((f32[8,14,8,128]{3,1,2,0:T(8,128)}), f32[1,14,8,128]{3,1,2,0:T(8,128)}) %reduce-scatter.2.cloned.1.call-update) | async-done | bytes 57360 | tf_op jit(solution)/shard_map/reduce_scatter | solution.py:118
  167.9 1.5 copy.14
  (68 shorter events, 4.6 us)
Async XLA Ops:
  7.2 90.6 %copy-start = (f32[8,14]{1,0:T(8,128)S(1)}, f32[8,14]{1,0:T(8,128)}, u32[]{:S(2)}) copy-start(f32[8,14]{1,0:T(8,128)} %param.16) | copy-start | bytes 1348
  7.2 41.8 %copy-start.1 = (f32[12,8,8,128]{3,2,1,0:T(8,128)S(1)}, f32[12,8,8,128]{3,2,1,0:T(8,128)}, u32[]{:S(2)}) copy-start(f32[12,8,8,128]{3,2,1,0:T(8,128)} %param.9) | copy-start | bytes 1179652
  7.2 160.7 %reduce-scatter.2.cloned.1.call-start = ((), (), s32[]{:S(2)}) async-start(), calls=%async_computation.1 | async-start | bytes 589824 | tf_op jit(solution)/shard_map/reduce_scatter | solution.py:118
  36.7 61.3 %collective-permute-start.1 = (f32[13,8,2,128]{3,2,1,0:T(2,128)S(1)}, f32[13,8,2,128]{3,2,1,0:T(2,128)S(1)}, u32[]{:S(2)}, u32[]{:S(2)}) collective-permute-start(f32[13,8,2,128]{3,2,1,0:T(2,128)S(1)} %get-tuple-element.32), channel_id=1, source_target_pairs={{8,0},{16,8},{24,16},{32,24},{40,32},{48,40},{56,48},{64,56},{72,6... | collective-permute-start | bytes 319496 | tf_op jit(solution)/shard_map/ppermute | solution.py:16
  47.0 50.9 %collective-permute-start = (f32[13,8,2,128]{3,2,1,0:T(2,128)S(1)}, f32[13,8,2,128]{3,2,1,0:T(2,128)S(1)}, u32[]{:S(2)}, u32[]{:S(2)}) collective-permute-start(f32[13,8,2,128]{3,2,1,0:T(2,128)S(1)} %get-tuple-element.31), channel_id=1, source_target_pairs={{0,8},{8,16},{16,24},{24,32},{32,40},{40,48},{48,56},{56,64},{64,7... | collective-permute-start | bytes 319496 | tf_op jit(solution)/shard_map/ppermute | solution.py:13
  49.2 0.7 copy-start.3
  65.7 0.7 copy-start.4
  81.5 14.7 %copy-start.6 = (s32[8,128]{1,0:T(8,128)S(1)}, s32[8,128]{1,0:T(8,128)}, u32[]{:S(2)}) copy-start(s32[8,128]{1,0:T(8,128)} %param.14) | copy-start | bytes 12292
  81.5 0.7 copy-start.5
  96.2 0.7 copy-start.7
  96.9 0.7 copy-start.8
  100.2 14.6 %collective-permute-start.3 = (f32[13,8,2,128]{3,2,1,0:T(2,128)S(1)}, f32[13,8,2,128]{3,2,1,0:T(2,128)S(1)}, u32[]{:S(2)}, u32[]{:S(2)}) collective-permute-start(f32[13,8,2,128]{3,2,1,0:T(2,128)S(1)} %get-tuple-element.30), channel_id=1, source_target_pairs={{8,0},{16,8},{24,16},{32,24},{40,32},{48,40},{56,48},{64,56},{72,6... | collective-permute-start | bytes 319496 | tf_op jit(solution)/shard_map/ppermute | solution.py:16
  111.7 14.7 %collective-permute-start.2 = (f32[13,8,2,128]{3,2,1,0:T(2,128)S(1)}, f32[13,8,2,128]{3,2,1,0:T(2,128)S(1)}, u32[]{:S(2)}, u32[]{:S(2)}) collective-permute-start(f32[13,8,2,128]{3,2,1,0:T(2,128)S(1)} %get-tuple-element.29), channel_id=1, source_target_pairs={{0,8},{8,16},{16,24},{24,32},{32,40},{40,48},{48,56},{56,64},{64,7... | collective-permute-start | bytes 319496 | tf_op jit(solution)/shard_map/ppermute | solution.py:13
  128.2 0.7 copy-start.2
Sparse Core Ops, SparseCore 0:
  130.6 37.1 reduce-scatter.1
where the time goes:
time: 177 us; the launch traced here: 176 us
  blocking collectives  72 us (41%)
  waiting for transfers between devices  49 us (28%)
  starting transfers between devices  25.8 us (15%)
  between operations  14.5 us (8%)
  local copies, waits for them, and re-layouts  6.68 us (4%)
  other arithmetic  6.2 us (4%)
  matrix products  1.96 us (1%)
    reduce_scatter x1, waiting for transfers between devices, local(): lax.psum_scatter(partial_sum, 'tracer', scatter_dimension=0, tiled=True)  37.3 us
    all_gather x1, blocking collectives, local(): lax.all_gather(courant_x, 'tracer', axis=0, tiled=True)  28.2 us
    ppermute x2, starting transfers between devices, with_halo(): lax.ppermute(lax.slice_in_dim(block, 0, width, axis=dim), axis, backward)  22 us
    all_gather x1, blocking collectives, local(): lax.all_gather(courant_y, 'tracer', axis=0, tiled=True)  15.8 us
    all_gather x1, blocking collectives, local(): lax.all_gather(humidity, 'tracer', axis=0, tiled=True)  14 us
    all_gather x1, blocking collectives, local(): lax.all_gather(kdiff, 'tracer', axis=0, tiled=True)  14 us
    ppermute x2, waiting for transfers between devices, with_halo(): lax.ppermute(lax.slice_in_dim(block, block.shape[dim] - width, None, axis...  11.7 us
    unnamed x25, local copies, waits for them, and re-layouts  5.24 us
  transfers between devices with their start and end apart: 5, of which 2 were waited for; matrix products, arithmetic and copies ran while one was open for 2% of the time, Pallas kernels for 0%

commit v1 on v0

v1 whole, which is shorter than its diff:
```python
import functools

import jax
import jax.numpy as jnp
from jax import lax
from jax.experimental import pallas as pl
from jax.experimental.pallas import tpu as pltpu
from jax.sharding import PartitionSpec as P

MESH = pl.DeviceIdType.MESH
F32 = jnp.float32
TR = 12
LEV = 8
ROWS = 8
NY = 128
NCLASS = 8
BANDS = 14
GROUP = 8
CHIPS = 4
PER = 3
CHUNKS = TR // PER

X0, XS0, XC, XSC, X1, XS1, GA, GB, HA, HB, YGA, YGB, YHA, YHB, INV, UP, LOW = range(17)
NCOEF = 17


def limited(near, far):
    return jnp.minimum(jnp.maximum(near, jnp.minimum(far, 0.0)), jnp.maximum(far, 0.0))


def roll_rows(a, by):
    return pltpu.roll(a, by % ROWS, 0)


def roll_lanes(a, by):
    return pltpu.roll(a, by % NY, 1)


def face_coefs(c):
    plus, minus = jnp.maximum(c, 0.0), jnp.minimum(c, 0.0)
    return plus, plus * (0.5 * (1.0 - c)), minus, minus * (-0.5 * (1.0 + c))


def kernel(
    tiles,
    x_hbm, cx_hbm, cy_hbm, kd_hbm, hum_hbm, land_hbm, cls_ref, opt_ref, hyg_ref,
    out_ref, ext_ref,
    ext, fields, kd, hum, land, coef, sbuf, spair, sx, sr, swell,
    ready, loc, own, hs, hr, es, er, gs, gr, ps, pr, xs, xr,
):
    me, k = lax.axis_index("tile"), lax.axis_index("tracer")
    right, left = lax.rem(me + 1, tiles), lax.rem(me + tiles - 1, tiles)
    chip, core = k // 2, lax.rem(k, 2)

    loads = [
        pltpu.make_async_copy(cx_hbm, fields.at[pl.ds(k, 1), 0, pl.ds(4, ROWS)], loc.at[0]),
        pltpu.make_async_copy(cy_hbm, fields.at[pl.ds(k, 1), 1, pl.ds(4, ROWS)], loc.at[1]),
        pltpu.make_async_copy(kd_hbm, kd, loc.at[2]),
        pltpu.make_async_copy(hum_hbm, hum, loc.at[3]),
        pltpu.make_async_copy(land_hbm, land, loc.at[4]),
    ]
    for copy in loads:
        copy.start()

    barrier = pltpu.get_barrier_semaphore()
    pl.semaphore_signal(barrier, inc=1, device_id=(left, k), device_id_type=MESH)
    for step in range(1, GROUP):
        pl.semaphore_signal(
            barrier, inc=1, device_id=(me, lax.rem(k + step, GROUP)), device_id_type=MESH
        )
    own_copy = pltpu.make_async_copy(x_hbm, ext.at[:, :, pl.ds(4, ROWS), :], own)
    own_copy.start()
    pl.semaphore_wait(barrier, GROUP)
    pl.semaphore_signal(ready, inc=1, device_id=(right, k), device_id_type=MESH)

    def halo(half, chunk):
        t = pl.ds(chunk * PER, PER)
        return pltpu.make_async_remote_copy(
            src_ref=x_hbm.at[t, :, pl.ds(4 - 4 * half, 4), :],
            dst_ref=ext.at[t, :, pl.ds(12 * half, 4), :],
            send_sem=hs.at[half, chunk],
            recv_sem=hr.at[half, chunk],
            device_id=((left if half else right), k),
            device_id_type=MESH,
        )

    def edge(half):
        src, dst, count = ((10, 2, 2), (4, 12, 4))[half]
        return pltpu.make_async_remote_copy(
            src_ref=fields.at[k, :, pl.ds(src, count), :],
            dst_ref=fields.at[k, :, pl.ds(dst, count), :],
            send_sem=es.at[half],
            recv_sem=er.at[half],
            device_id=((left if half else right), k),
            device_id_type=MESH,
        )

    def spread(part, step):
        first, count = ((2, 2), (12, 4), (4, ROWS))[part]
        return pltpu.make_async_remote_copy(
            src_ref=fields.at[k, :, pl.ds(first, count), :],
            dst_ref=fields.at[k, :, pl.ds(first, count), :],
            send_sem=gs.at[part, step],
            recv_sem=gr.at[part, k],
            device_id=(me, lax.rem(k + step, GROUP)),
            device_id_type=MESH,
        )

    def spread_wait(part, step):
        first, count = ((2, 2), (12, 4), (4, ROWS))[part]
        other = lax.rem(k + step, GROUP)
        pltpu.make_async_remote_copy(
            src_ref=fields.at[other, :, pl.ds(first, count), :],
            dst_ref=fields.at[other, :, pl.ds(first, count), :],
            send_sem=gs.at[part, step],
            recv_sem=gr.at[part, other],
            device_id=(me, other),
            device_id_type=MESH,
        ).wait_recv()

    halo(0, 0).start()
    for copy in loads:
        copy.wait()
    lowest = jnp.where(k == LEV - 1, 1.0, 0.0).astype(F32)
    fields[k, 2, pl.ds(4, ROWS), :] = kd[0] * (
        1.0 + lowest * (0.25 + 0.75 * land[...].astype(F32) - 1.0)
    )
    edge(0).start()
    for step in range(1, GROUP):
        spread(2, step).start()
    for chunk in range(1, CHUNKS):
        halo(0, chunk).start()

    dryness = jnp.log(1.0 - hum[0])
    for c in range(NCLASS):
        swell[c] = jnp.exp(-hyg_ref[c] * dryness)

    pl.semaphore_wait(ready, 1)
    edge(1).start()
    for chunk in range(CHUNKS):
        halo(1, chunk).start()

    for half in (1, 0):
        edge(half).wait_recv()
        for step in range(1, GROUP):
            spread(half, step).start()
    for part in (2, 1, 0):
        for step in range(1, GROUP):
            spread_wait(part, step)

    def coefficients(half):
        base = 4 * half
        upper = previous = None
        for level in range(LEV):
            p0, r0, q0, t0 = face_coefs(fields[level, 0, pl.ds(base + 2, ROWS), :])
            p1, r1, q1, t1 = face_coefs(fields[level, 0, pl.ds(base + 3, ROWS), :])
            put = lambda row, value: coef.__setitem__((half, level, row), value)
            put(X0, p0)
            put(XS0, r0)
            put(XC, 1.0 + q0 - p1)
            put(XSC, t0 - r1)
            put(X1, -q1)
            put(XS1, -t1)
            put(GA, p1)
            put(GB, r1)
            put(HA, q0)
            put(HB, t0)
            yp, yr, yq, yt = face_coefs(fields[level, 1, pl.ds(base + 2, ROWS), :])
            put(YGA, roll_lanes(yp, -1))
            put(YGB, roll_lanes(yr, -1))
            put(YHA, yq)
            put(YHB, yt)
            lower = fields[level, 2, pl.ds(base + 2, ROWS), :]
            if level == 0:
                inverse = 1.0 / (1.0 + lower)
                put(UP, jnp.zeros_like(inverse))
            else:
                inverse = 1.0 / (1.0 + upper + lower - upper * previous)
                put(UP, upper * inverse)
            previous = lower * inverse
            upper = lower
            put(INV, inverse)
            put(LOW, previous)

    coefficients(1)
    coefficients(0)
    own_copy.wait()

    def mixed(moved, half):
        forward = []
        for level in range(LEV):
            solved = moved[level] * coef[half, level, INV]
            if level:
                solved = solved + coef[half, level, UP] * forward[-1]
            forward.append(solved)
        for level in range(LEV - 2, -1, -1):
            forward[level] = forward[level] + coef[half, level, LOW] * forward[level + 1]
        return forward

    def along_y(v, half, level):
        jump = v - roll_lanes(v, 1)
        slope = limited(jump, roll_lanes(jump, -1))
        ahead = coef[half, level, YGA] * v + coef[half, level, YGB] * slope
        flux = roll_lanes(ahead, 1) + coef[half, level, YHA] * v + coef[half, level, YHB] * slope
        return flux - roll_lanes(flux, -1)

    def two_steps(t, half):
        base = 4 * half
        moved = []
        for level in range(LEV):
            v = [ext[t, level, pl.ds(base + n, ROWS), :] for n in range(5)]
            jump = [v[n + 1] - v[n] for n in range(4)]
            slope = [limited(jump[n], jump[n + 1]) for n in range(3)]
            c = lambda row: coef[half, level, row]
            moved.append(
                (c(X0) * v[1] + c(XS0) * slope[0])
                + (c(XC) * v[2] + c(XSC) * slope[1])
                + (c(X1) * v[3] + c(XS1) * slope[2])
                + along_y(v[2], half, level)
            )
        middle = mixed(moved, half)
        moved = []
        for level in range(LEV):
            m = middle[level]
            c = lambda row: coef[half, level, row]
            jump = m - roll_rows(m, 1)
            slope = limited(jump, roll_rows(jump, -1))
            flux = roll_rows(c(GA) * m + c(GB) * slope, 1) + c(HA) * m + c(HB) * slope
            moved.append(m + flux - roll_rows(flux, -1) + along_y(m, half, level))
        final = mixed(moved, half)
        for level in range(LEV):
            out_ref[t, level, pl.ds(base, 4), :] = final[level][2:6, :]

    def do_chunk(half, chunk):
        halo(half ^ 0, chunk).wait_recv()
        first = chunk * PER

        def body(i, carry):
            two_steps(first + i, half)
            return carry

        lax.fori_loop(0, PER, body, 0)
        rows = pl.ds(4 * half, 4)
        weights = []
        for i in range(PER):
            own_class = cls_ref[k * TR + first + i]
            weights.append([jnp.where(own_class == c, 1.0, 0.0).astype(F32) for c in range(NCLASS)])
        for level in range(LEV):
            values = [out_ref[first + i, level, rows, :] for i in range(PER)]
            at = (level % 2, level // 2)
            for c in range(NCLASS):
                total = sum(weights[i][c] * values[i] for i in range(PER))
                if chunk:
                    total = total + sbuf[at[0], at[1], c, rows, :]
                sbuf[at[0], at[1], c, rows, :] = total

    def pair(half, step):
        to = lax.rem(chip + step, CHIPS)
        rows = pl.ds(4 * half, 4)
        return pltpu.make_async_remote_copy(
            src_ref=sbuf.at[1 - core, to, :, rows, :],
            dst_ref=spair.at[to, :, rows, :],
            send_sem=ps.at[half, step],
            recv_sem=pr.at[half, step],
            device_id=(me, 2 * chip + 1 - core),
            device_id_type=MESH,
        )

    def cross(half, step):
        to = lax.rem(chip + step, CHIPS)
        rows = pl.ds(4 * half, 4)
        return pltpu.make_async_remote_copy(
            src_ref=sx.at[to, :, rows, :],
            dst_ref=sr.at[step, :, rows, :],
            send_sem=xs.at[half, step],
            recv_sem=xr.at[half, step],
            device_id=(me, 2 * to + core),
            device_id_type=MESH,
        )

    def start_pair(half):
        for step in (2, 1, 3, 0):
            pair(half, step).start()

    def start_cross(half):
        rows = pl.ds(4 * half, 4)
        for step in (2, 1, 3, 0):
            pair(half, step).wait_recv()
            to = lax.rem(chip + step, CHIPS)
            sx[to, :, rows, :] = sbuf[core, to, :, rows, :] + spair[to, :, rows, :]
            if step:
                cross(half, step).start()

    for chunk in range(CHUNKS):
        do_chunk(1, chunk)
    start_pair(1)
    for chunk in range(CHUNKS):
        do_chunk(0, chunk)
        if chunk == 0:
            start_cross(1)
    start_pair(0)
    start_cross(0)
    for half in (1, 0):
        for step in range(1, CHIPS):
            cross(half, step).wait_recv()
    wetted = []
    for c in range(NCLASS):
        total = (sx[chip, c] + sr[1, c]) + (sr[2, c] + sr[3, c])
        wetted.append(total * swell[c])
    for b in range(BANDS):
        ext_ref[0, b] = sum(opt_ref[c, b] * wetted[c] for c in range(NCLASS))

    for half in (0, 1):
        edge(half).wait_send()
        for chunk in range(CHUNKS):
            halo(half, chunk).wait_send()
        for step in range(CHIPS):
            pair(half, step).wait_send()
            if step:
                cross(half, step).wait_send()
    for part in range(3):
        for step in range(1, GROUP):
            spread(part, step).wait_send()


def local(tiles, tracers, courant_x, courant_y, kdiff, humidity, land, band_class, opt_table, hyg_table):
    hbm = pl.BlockSpec(memory_space=pltpu.HBM)
    vmem = pl.BlockSpec(memory_space=pltpu.VMEM)
    smem = pl.BlockSpec(memory_space=pltpu.SMEM)
    dma = pltpu.SemaphoreType.DMA
    return tuple(
        pl.pallas_call(
            functools.partial(kernel, tiles),
            out_shape=(
                jax.ShapeDtypeStruct((TR, LEV, ROWS, NY), F32),
                jax.ShapeDtypeStruct((1, BANDS, ROWS, NY), F32),
            ),
            in_specs=[hbm] * 6 + [smem] * 3,
            out_specs=(vmem, vmem),
            scratch_shapes=[
                pltpu.VMEM((TR, LEV, 16, NY), F32),
                pltpu.VMEM((LEV, 3, 16, NY), F32),
                pltpu.VMEM((1, ROWS, NY), F32),
                pltpu.VMEM((1, ROWS, NY), F32),
                pltpu.VMEM((ROWS, NY), jnp.int32),
                pltpu.VMEM((2, LEV, NCOEF, ROWS, NY), F32),
                pltpu.VMEM((2, CHIPS, NCLASS, ROWS, NY), F32),
                pltpu.VMEM((CHIPS, NCLASS, ROWS, NY), F32),
                pltpu.VMEM((CHIPS, NCLASS, ROWS, NY), F32),
                pltpu.VMEM((CHIPS, NCLASS, ROWS, NY), F32),
                pltpu.VMEM((NCLASS, ROWS, NY), F32),
                pltpu.SemaphoreType.REGULAR,
                dma((5,)),
                dma,
                dma((2, CHUNKS)),
                dma((2, CHUNKS)),
                dma((2,)),
                dma((2,)),
                dma((3, GROUP)),
                dma((3, GROUP)),
                dma((2, CHIPS)),
                dma((2, CHIPS)),
                dma((2, CHIPS)),
                dma((2, CHIPS)),
            ],
            compiler_params=pltpu.CompilerParams(
                collective_id=0, has_side_effects=True, vmem_limit_bytes=32 << 20
            ),
        )(tracers, courant_x, courant_y, kdiff, humidity, land, band_class, opt_table, hyg_table)
    )


def solution(mesh):
    in_specs = (
        P("tracer", None, "tile", None),
        P("tracer", "tile", None),
        P("tracer", "tile", None),
        P("tracer", "tile", None),
        P("tracer", "tile", None),
        P("tile", None),
        P(),
        P(),
        P(),
    )
    out_specs = (P("tracer", None, "tile", None), P("tracer", None, "tile", None))
    return jax.shard_map(
        functools.partial(local, mesh.shape["tile"]),
        mesh=mesh, in_specs=in_specs, out_specs=out_specs, check_vma=False,
    )
```

time: 177 us -> 71.5 us (0.40)
  blocking collectives: 72 us -> 0 us
  Pallas kernels: 0 us -> 62.7 us
  waiting for transfers between devices: 49 us -> 0 us
  starting transfers between devices: 25.8 us -> 0 us
  between operations: 14.5 us -> 0.66 us
  other arithmetic: 6.2 us -> 0 us
  matrix products: 1.96 us -> 0 us
    all_gather x4 -> x0, blocking collectives: 72 us -> none  [the longest x1 28.2 us: local(): lax.all_gather(courant_x, 'tracer', axis=0, tiled=True)]
    pallas_call x0 -> x1, Pallas kernels: none -> 62.7 us  [local(): pl.pallas_call(functools.partial(kernel, tiles), out_shape=(jax.ShapeDtyp...]
    reduce_scatter x1 -> x0, waiting for transfers between devices: 37.3 us -> none  [local(): lax.psum_scatter(partial_sum, 'tracer', scatter_dimension=0, tiled=True)]
    ppermute x4 -> x0, starting transfers between devices: 25.8 us -> none  [the longest x2 22 us: with_halo(): lax.ppermute(lax.slice_in_dim(block, 0, width, axis=dim), axis, backward)]
    ppermute x4 -> x0, waiting for transfers between devices: 11.7 us -> none  [the longest x2 11.7 us: with_halo(): lax.ppermute(lax.slice_in_dim(block, block.shape[dim] - width, None, axis...]
    mul x13 -> x0, other arithmetic: 3.52 us -> none  [the longest x4 1.99 us: minmod(): 0.5 * (jnp.sign(left_step) + jnp.sign(right_step))]
    unnamed x25 -> x20, local copies, waits for them, and re-layouts: 5.24 us -> 7.79 us
    dot_general x3 -> x0, matrix products: 1.96 us -> none  [the longest x1 1.58 us: local(): jnp.einsum('tlxy,tb->lbxy', wetted, optics, precision=lax.Precision.HIGHEST)]
  transfers between devices with their start and end apart: 5 -> 0, of which waited for: 2 -> 0; matrix products, arithmetic and copies ran while one was open for 2% -> 0% of each run, Pallas kernels for 0% -> 0%
where the time goes in v1:
time: 71.5 us; the launch traced here: 71.1 us
  Pallas kernels  62.7 us (88%)
  local copies, waits for them, and re-layouts  7.79 us (11%)
    pallas_call x1, Pallas kernels, local(): pl.pallas_call(functools.partial(kernel, tiles), out_shape=(jax.ShapeDtyp...  62.7 us
    unnamed x20, local copies, waits for them, and re-layouts  7.79 us

profile of v1, /device:TPU:1, one launch (start us, length us, event | category | flops | bytes accessed | tf_op | source)
XLA Modules:
  0.0 71.1 jit_solution(7785165662582724751)
XLA Ops:
  0.6 0.0 copy-start
  0.6 1.0 %copy-done = f32[12,8,8,128]{3,2,1,0:T(8,128)S(1)} copy-done((f32[12,8,8,128]{3,2,1,0:T(8,128)S(1)}, f32[12,8,8,128]{3,2,1,0:T(8,128)}, u32[]{:S(2)}) %copy-start) | copy-done | bytes 393240
  1.6 0.0 copy-start.1
  1.6 0.7 copy-done.1
  2.3 0.0 copy-start.2
  2.3 0.7 copy-done.2
  3.0 0.0 copy-start.3
  3.0 0.7 copy-done.3
  3.7 0.0 copy-start.4
  3.7 0.7 copy-done.4
  4.4 0.0 copy-start.5
  4.4 0.7 copy-done.5
  5.1 0.0 copy-start.6
  5.1 0.7 copy-done.6
  5.8 0.0 copy-start.7
  5.8 0.7 copy-done.7
  6.4 0.0 copy-start.8
  6.4 0.7 copy-done.8
  7.1 62.7 %shard_map.104 = (f32[12,8,8,128]{3,2,1,0:T(8,128)S(1)}, f32[1,14,8,128]{3,2,1,0:T(8,128)S(1)}) custom-call(f32[12,8,8,128]{3,2,1,0:T(8,128)S(1)} %copy-done, f32[1,8,128]{2,1,0:T(8,128)S(1)} %copy-done.1, f32[1,8,128]{2,1,0:T(8,128)S(1)} %copy-done.2, f32[1,8,128]{2,1,0:T(8,128)S(1)} %copy-done.3, f32[1,8,128]{2,1,0:T(8,128)S(1)} %copy-done.4, ...), custom_call_target="tpu_custom_call" | custom-call | tf_op jit(solution)/shard_map/pallas_call | solution.py:332
  69.8 0.7 %copy.13 = f32[12,8,8,128]{3,2,1,0:T(8,128)} copy(f32[12,8,8,128]{3,2,1,0:T(8,128)S(1)} %get-tuple-element.4) | data formatting | bytes 786432
  70.5 0.6 copy.14
Async XLA Ops:
  0.6 1.0 %copy-start = (f32[12,8,8,128]{3,2,1,0:T(8,128)S(1)}, f32[12,8,8,128]{3,2,1,0:T(8,128)}, u32[]{:S(2)}) copy-start(f32[12,8,8,128]{3,2,1,0:T(8,128)} %x_hbm.1) | copy-start | bytes 1179652
  1.6 0.7 copy-start.1
  2.3 0.7 copy-start.2
  3.0 0.7 copy-start.3
  3.7 0.7 copy-start.4
  4.4 0.7 copy-start.5
  5.1 0.7 copy-start.6
  5.8 0.7 copy-start.7
  6.4 0.7 copy-start.8

commit v2 on v1

--- a/solution.py
+++ b/solution.py
@@ -20,8 +20,9 @@
 PER = 3
 CHUNKS = TR // PER
 
-X0, XS0, XC, XSC, X1, XS1, GA, GB, HA, HB, YGA, YGB, YHA, YHB, INV, UP, LOW = range(17)
-NCOEF = 17
+V, V2, XJ0, XJ1, XS0, XS1, XS2, GA, GB, HA, HB, YJ0, YJ1, YS0, YS1, YS2, INV, UP, LOW = range(19)
+NCOEF = 19
+ROWS_CHUNK = PER * LEV * ROWS
 
 
 def limited(near, far):
@@ -45,7 +46,7 @@
     tiles,
     x_hbm, cx_hbm, cy_hbm, kd_hbm, hum_hbm, land_hbm, cls_ref, opt_ref, hyg_ref,
     out_ref, ext_ref,
-    ext, fields, kd, hum, land, coef, sbuf, spair, sx, sr, swell,
+    ext, fields, kd, hum, land, coef, shift, jumps, middle_ref, sbuf, spair, sx, sr, swell,
     ready, loc, own, hs, hr, es, er, gs, gr, ps, pr, xs, xr,
 ):
     me, k = lax.axis_index("tile"), lax.axis_index("tracer")
@@ -148,28 +149,43 @@
         for step in range(1, GROUP):
             spread_wait(part, step)
 
+    from_y = lax.broadcasted_iota(jnp.int32, (2 * NY, NY), 0) % NY
+    to_y = lax.broadcasted_iota(jnp.int32, (2 * NY, NY), 1)
+    for n in range(4):
+        plus = jnp.where(from_y == (to_y + n + NY - 1) % NY, 1.0, 0.0)
+        minus = jnp.where(from_y == (to_y + n + NY - 2) % NY, 1.0, 0.0)
+        shift[:, pl.ds(n * NY, NY)] = (plus - minus).astype(jnp.bfloat16)
+    sbuf[...] = jnp.zeros_like(sbuf)
+
     def coefficients(half):
         base = 4 * half
         upper = previous = None
         for level in range(LEV):
-            p0, r0, q0, t0 = face_coefs(fields[level, 0, pl.ds(base + 2, ROWS), :])
-            p1, r1, q1, t1 = face_coefs(fields[level, 0, pl.ds(base + 3, ROWS), :])
+            c0 = fields[level, 0, pl.ds(base + 2, ROWS), :]
+            c1 = fields[level, 0, pl.ds(base + 3, ROWS), :]
+            p0, r0, q0, t0 = face_coefs(c0)
+            p1, r1, q1, t1 = face_coefs(c1)
             put = lambda row, value: coef.__setitem__((half, level, row), value)
-            put(X0, p0)
+            put(XJ0, -p0)
+            put(XJ1, -q1)
             put(XS0, r0)
-            put(XC, 1.0 + q0 - p1)
-            put(XSC, t0 - r1)
-            put(X1, -q1)
-            put(XS1, -t1)
+            put(XS1, t0 - r1)
+            put(XS2, -t1)
             put(GA, p1)
             put(GB, r1)
             put(HA, q0)
             put(HB, t0)
-            yp, yr, yq, yt = face_coefs(fields[level, 1, pl.ds(base + 2, ROWS), :])
-            put(YGA, roll_lanes(yp, -1))
-            put(YGB, roll_lanes(yr, -1))
-            put(YHA, yq)
-            put(YHB, yt)
+            d0 = fields[level, 1, pl.ds(base + 2, ROWS), :]
+            d1 = roll_lanes(d0, -1)
+            put(V, 1.0 + (c0 - c1) + (d0 - d1))
+            put(V2, 1.0 + (d0 - d1))
+            p0, r0, q0, t0 = face_coefs(d0)
+            p1, r1, q1, t1 = face_coefs(d1)
+            put(YJ0, -p0)
+            put(YJ1, -q1)
+            put(YS0, r0)
+            put(YS1, t0 - r1)
+            put(YS2, -t1)
             lower = fields[level, 2, pl.ds(base + 2, ROWS), :]
             if level == 0:
                 inverse = 1.0 / (1.0 + lower)
@@ -197,49 +213,73 @@
             forward[level] = forward[level] + coef[half, level, LOW] * forward[level + 1]
         return forward
 
-    def along_y(v, half, level):
-        jump = v - roll_lanes(v, 1)
-        slope = limited(jump, roll_lanes(jump, -1))
-        ahead = coef[half, level, YGA] * v + coef[half, level, YGB] * slope
-        flux = roll_lanes(ahead, 1) + coef[half, level, YHA] * v + coef[half, level, YHB] * slope
-        return flux - roll_lanes(flux, -1)
-
-    def two_steps(t, half):
+    def jumps_along_y(v):
+        lead = v.astype(jnp.bfloat16)
+        trail = (v - lead.astype(F32)).astype(jnp.bfloat16)
+        jumps[...] = jnp.dot(
+            jnp.concatenate([lead, trail], 1), shift[...], preferred_element_type=F32
+        )
+
+    def along_y(row, c):
+        jump = [jumps[pl.ds(row, ROWS), pl.ds(n * NY, NY)] for n in range(4)]
+        slope = [limited(jump[n], jump[n + 1]) for n in range(3)]
+        return (
+            (c(YJ0) * jump[1] + c(YJ1) * jump[2])
+            + (c(YS0) * slope[0] + c(YS1) * slope[1])
+            + c(YS2) * slope[2]
+        )
+
+    def first_step(i, t, half):
         base = 4 * half
         moved = []
         for level in range(LEV):
+            c = lambda row: coef[half, level, row]
             v = [ext[t, level, pl.ds(base + n, ROWS), :] for n in range(5)]
             jump = [v[n + 1] - v[n] for n in range(4)]
             slope = [limited(jump[n], jump[n + 1]) for n in range(3)]
+            row = pl.multiple_of((i * LEV + level) * ROWS, ROWS)
+            moved.append(
+                (c(V) * v[2] + c(XJ0) * jump[1])
+                + (c(XJ1) * jump[2] + c(XS0) * slope[0])
+                + (c(XS1) * slope[1] + c(XS2) * slope[2])
+                + along_y(row, c)
+            )
+        moved = mixed(moved, half)
+        for level in range(LEV):
+            row = pl.multiple_of((i * LEV + level) * ROWS, ROWS)
+            middle_ref[pl.ds(row, ROWS), :] = moved[level]
+
+    def second_step(i, t, half):
+        moved = []
+        for level in range(LEV):
             c = lambda row: coef[half, level, row]
-            moved.append(
-                (c(X0) * v[1] + c(XS0) * slope[0])
-                + (c(XC) * v[2] + c(XSC) * slope[1])
-                + (c(X1) * v[3] + c(XS1) * slope[2])
-                + along_y(v[2], half, level)
-            )
-        middle = mixed(moved, half)
-        moved = []
-        for level in range(LEV):
-            m = middle[level]
-            c = lambda row: coef[half, level, row]
+            row = pl.multiple_of((i * LEV + level) * ROWS, ROWS)
+            m = middle_ref[pl.ds(row, ROWS), :]
             jump = m - roll_rows(m, 1)
             slope = limited(jump, roll_rows(jump, -1))
             flux = roll_rows(c(GA) * m + c(GB) * slope, 1) + c(HA) * m + c(HB) * slope
-            moved.append(m + flux - roll_rows(flux, -1) + along_y(m, half, level))
+            moved.append((c(V2) * m + flux) - roll_rows(flux, -1) + along_y(row, c))
         final = mixed(moved, half)
         for level in range(LEV):
-            out_ref[t, level, pl.ds(base, 4), :] = final[level][2:6, :]
+            out_ref[t, level, pl.ds(4 * half, 4), :] = final[level][2:6, :]
 
     def do_chunk(half, chunk):
-        halo(half ^ 0, chunk).wait_recv()
+        halo(half, chunk).wait_recv()
         first = chunk * PER
-
-        def body(i, carry):
-            two_steps(first + i, half)
+        own_rows = ext[pl.ds(first, PER), :, pl.ds(4 * half + 2, ROWS), :]
+        jumps_along_y(own_rows.reshape(ROWS_CHUNK, NY))
+
+        def first_body(i, carry):
+            first_step(i, first + i, half)
             return carry
 
-        lax.fori_loop(0, PER, body, 0)
+        def second_body(i, carry):
+            second_step(i, first + i, half)
+            return carry
+
+        lax.fori_loop(0, PER, first_body, 0)
+        jumps_along_y(middle_ref[...])
+        lax.fori_loop(0, PER, second_body, 0)
         rows = pl.ds(4 * half, 4)
         weights = []
         for i in range(PER):
@@ -250,9 +290,7 @@
             at = (level % 2, level // 2)
             for c in range(NCLASS):
                 total = sum(weights[i][c] * values[i] for i in range(PER))
-                if chunk:
-                    total = total + sbuf[at[0], at[1], c, rows, :]
-                sbuf[at[0], at[1], c, rows, :] = total
+                sbuf[at[0], at[1], c, rows, :] = sbuf[at[0], at[1], c, rows, :] + total
 
     def pair(half, step):
         to = lax.rem(chip + step, CHIPS)
@@ -291,13 +329,22 @@
             if step:
                 cross(half, step).start()
 
-    for chunk in range(CHUNKS):
+    def after_body(chunk, carry):
         do_chunk(1, chunk)
+        return carry
+
+    def before_body(chunk, carry):
+        do_chunk(0, chunk)
+
+        @pl.when(chunk == 0)
+        def _():
+            start_cross(1)
+
+        return carry
+
+    lax.fori_loop(0, CHUNKS, after_body, 0)
     start_pair(1)
-    for chunk in range(CHUNKS):
-        do_chunk(0, chunk)
-        if chunk == 0:
-            start_cross(1)
+    lax.fori_loop(0, CHUNKS, before_body, 0)
     start_pair(0)
     start_cross(0)
     for half in (1, 0):
@@ -344,6 +391,9 @@
                 pltpu.VMEM((1, ROWS, NY), F32),
                 pltpu.VMEM((ROWS, NY), jnp.int32),
                 pltpu.VMEM((2, LEV, NCOEF, ROWS, NY), F32),
+                pltpu.VMEM((2 * NY, 4 * NY), jnp.bfloat16),
+                pltpu.VMEM((ROWS_CHUNK, 4 * NY), F32),
+                pltpu.VMEM((ROWS_CHUNK, NY), F32),
                 pltpu.VMEM((2, CHIPS, NCLASS, ROWS, NY), F32),
                 pltpu.VMEM((CHIPS, NCLASS, ROWS, NY), F32),
                 pltpu.VMEM((CHIPS, NCLASS, ROWS, NY), F32),
@@ -364,7 +414,7 @@
                 dma((2, CHIPS)),
             ],
             compiler_params=pltpu.CompilerParams(
-                collective_id=0, has_side_effects=True, vmem_limit_bytes=32 << 20
+                collective_id=0, has_side_effects=True, vmem_limit_bytes=63 << 20
             ),
         )(tracers, courant_x, courant_y, kdiff, humidity, land, band_class, opt_table, hyg_table)
     )

time: 71.5 us -> 59.2 us (0.83)
  Pallas kernels: 62.7 us -> 55.9 us
  local copies, waits for them, and re-layouts: 7.79 us -> 2.41 us
    pallas_call x1, Pallas kernels: 62.7 us -> 55.9 us  [local(): pl.pallas_call(functools.partial(kernel, tiles), out_shape=(jax.ShapeDtyp...]
    unnamed x20 -> x4, local copies, waits for them, and re-layouts: 7.79 us -> 2.41 us
where the time goes in v2:
time: 59.2 us; the launch traced here: 59 us
  Pallas kernels  55.9 us (94%)
  local copies, waits for them, and re-layouts  2.41 us (4%)
  between operations  0.65 us (1%)
    pallas_call x1, Pallas kernels, local(): pl.pallas_call(functools.partial(kernel, tiles), out_shape=(jax.ShapeDtyp...  55.9 us
    unnamed x4, local copies, waits for them, and re-layouts  2.41 us

profile of v2, /device:TPU:1, one launch (start us, length us, event | category | flops | bytes accessed | tf_op | source)
XLA Modules:
  0.0 59.0 jit_solution(5103905108594737310)
XLA Ops:
  0.6 55.9 %shard_map.104 = (f32[12,8,8,128]{3,2,1,0:T(8,128)}, f32[1,14,8,128]{3,2,1,0:T(8,128)}) custom-call(f32[12,8,8,128]{3,2,1,0:T(8,128)} %x_hbm.1, f32[1,8,128]{2,1,0:T(8,128)} %cx_hbm.1, f32[1,8,128]{2,1,0:T(8,128)} %cy_hbm.1, f32[1,8,128]{2,1,0:T(8,128)} %kd_hbm.1, f32[1,8,128]{2,1,0:T(8,128)} %hum_hbm.1, s32[8,128]{1,0:T(8,128)} %land_hbm.1, s32[96]{0:T(128)} %cls_ref.1, ...), custom_call_target="tpu_custom_call" | custom-call | tf_op jit(solution)/shard_map/pallas_call | solution.py:379
  56.6 0.0 copy-start
  56.6 1.8 %copy.13 = f32[12,8,8,128]{3,2,1,0:T(8,128)} copy(f32[12,8,8,128]{3,2,1,0:T(8,128)} %get-tuple-element.4) | data formatting | bytes 786432
  58.4 0.0 copy-done
  58.4 0.6 %copy.14 = f32[1,14,8,128]{3,2,1,0:T(8,128)} copy(f32[1,14,8,128]{3,2,1,0:T(8,128)S(1)} %copy-done) | data formatting | bytes 114688
Async XLA Ops:
  56.6 1.8 %copy-start = (f32[1,14,8,128]{3,2,1,0:T(8,128)S(1)}, f32[1,14,8,128]{3,2,1,0:T(8,128)}, u32[]{:S(2)}) copy-start(f32[1,14,8,128]{3,2,1,0:T(8,128)} %get-tuple-element.5) | copy-start | bytes 172036

commit v3 on v2

--- a/solution.py
+++ b/solution.py
@@ -17,7 +17,7 @@
 BANDS = 14
 GROUP = 8
 CHIPS = 4
-PER = 3
+PER = 6
 CHUNKS = TR // PER
 
 V, V2, XJ0, XJ1, XS0, XS1, XS2, GA, GB, HA, HB, YJ0, YJ1, YS0, YS1, YS2, INV, UP, LOW = range(19)

time: 59.2 us -> 58.2 us (0.983)
  Pallas kernels: 55.9 us -> 54.9 us
    pallas_call x1, Pallas kernels: 55.9 us -> 54.9 us  [local(): pl.pallas_call(functools.partial(kernel, tiles), out_shape=(jax.ShapeDtyp...]
where the time goes in v3:
time: 58.2 us; the launch traced here: 58 us
  Pallas kernels  54.9 us (94%)
  local copies, waits for them, and re-layouts  2.41 us (4%)
  between operations  0.65 us (1%)
    pallas_call x1, Pallas kernels, local(): pl.pallas_call(functools.partial(kernel, tiles), out_shape=(jax.ShapeDtyp...  54.9 us
    unnamed x4, local copies, waits for them, and re-layouts  2.41 us

profile of v3, /device:TPU:1, one launch (start us, length us, event | category | flops | bytes accessed | tf_op | source)
XLA Modules:
  0.0 58.0 jit_solution(6402970674643085325)
XLA Ops:
  0.6 54.9 %shard_map.104 = (f32[12,8,8,128]{3,2,1,0:T(8,128)}, f32[1,14,8,128]{3,2,1,0:T(8,128)}) custom-call(f32[12,8,8,128]{3,2,1,0:T(8,128)} %x_hbm.1, f32[1,8,128]{2,1,0:T(8,128)} %cx_hbm.1, f32[1,8,128]{2,1,0:T(8,128)} %cy_hbm.1, f32[1,8,128]{2,1,0:T(8,128)} %kd_hbm.1, f32[1,8,128]{2,1,0:T(8,128)} %hum_hbm.1, s32[8,128]{1,0:T(8,128)} %land_hbm.1, s32[96]{0:T(128)} %cls_ref.1, ...), custom_call_target="tpu_custom_call" | custom-call | tf_op jit(solution)/shard_map/pallas_call | solution.py:379
  55.6 0.0 copy-start
  55.6 1.8 %copy.13 = f32[12,8,8,128]{3,2,1,0:T(8,128)} copy(f32[12,8,8,128]{3,2,1,0:T(8,128)} %get-tuple-element.4) | data formatting | bytes 786432
  57.4 0.0 copy-done
  57.4 0.6 %copy.14 = f32[1,14,8,128]{3,2,1,0:T(8,128)} copy(f32[1,14,8,128]{3,2,1,0:T(8,128)S(1)} %copy-done) | data formatting | bytes 114688
Async XLA Ops:
  55.6 1.8 %copy-start = (f32[1,14,8,128]{3,2,1,0:T(8,128)S(1)}, f32[1,14,8,128]{3,2,1,0:T(8,128)}, u32[]{:S(2)}) copy-start(f32[1,14,8,128]{3,2,1,0:T(8,128)} %get-tuple-element.5) | copy-start | bytes 172036
